TPU v7x, 256 devices: a whole 4x4x8 slice. The times are simulated.
256 devices in a mesh: section: 4 (over y), expert: 64 (over x, z, core).
Axes of the slice: x: 4, y: 4, z: 8, core: 2. Of those that a mesh axis runs over, the one named last changes fastest.
Arguments:
- tokens_in: bfloat16 [4, 2048, 3584], P('section', 'expert'), may hold values from -6 to 6
- cotangent: bfloat16 [4, 2048, 3584], P('section', 'expert'), may hold values from -6 to 6
- norm_gain: float32 [4, 3584], P('section'), may hold values from 0.1 to 1.9
- w_gate: bfloat16 [4, 64, 3584, 512], P('section', 'expert'), may hold values from -0.09375 to 0.09375
- w_up: bfloat16 [4, 64, 3584, 512], P('section', 'expert'), may hold values from -0.09375 to 0.09375
- w_down: bfloat16 [4, 64, 512, 3584], P('section', 'expert'), may hold values from -0.1875 to 0.1875
- expert_ids: int32 [4, 4, 2048, 1], P('section', None, 'expert'), may hold values from 0 to 31; in each aligned block of 32 rows (0 to 31, 32 to 63, ..., all dimensions but the last counted through in order) at most 2 rows name the same one
- gate_weights: float32 [4, 4, 2048, 1], P('section', None, 'expert'), may hold values from 0.2 to 1
Outputs:
- grad_inputs: bfloat16 [4, 4, 2048, 3584], P('section', None, 'expert')
- grad_gates: float32 [4, 4, 2048, 1], P('section', None, 'expert')
Inputs may be any that keep to these rules, and one draw needn't show every extreme that they name: `expert_ids`: within each aligned block of 32 tokens of one layer and micro-batch no expert is named more than 2 times, a bound that some block reaches; each token names one expert.
All inputs are finite; a program needn't handle non-finite values.
Results may differ from a plain program's by a relative error of at most 0.025.
Values may be sent and summed in bfloat16 or wider, within the bound.
A program may use at most 192 MiB of HBM per device.

v0:
```python
from functools import partial

import jax
import jax.numpy as jnp
from jax import lax
from jax.sharding import PartitionSpec as P

epsilon = 1e-06


def shifted(block, axis, distance):
    devices = range(lax.axis_size(axis))
    route = [(i - distance, i) for i in devices if i - distance in devices]
    return lax.ppermute(block, axis, route)


def table_for(route_ids, expert_count, capacity):
    flat_ids = route_ids.reshape(-1)
    one_hot = (flat_ids[:, None] == jnp.arange(expert_count, dtype=jnp.int32)[None, :]).astype(
        jnp.int32
    )
    position = jnp.sum(
        (jnp.cumsum(one_hot, axis=0, dtype=jnp.int32) - 1) * one_hot, axis=-1, dtype=jnp.int32
    )
    slot_index = flat_ids * capacity + position
    place_table = (
        jnp.arange(expert_count * capacity, dtype=jnp.int32)[:, None] == slot_index[None, :]
    ).astype(jnp.bfloat16)
    return (slot_index, place_table)


def pick_entry(stored, chosen):
    return lax.dynamic_index_in_dim(stored, chosen, 0, keepdims=False)


def put_entry(stored, value, chosen, active):
    former = lax.dynamic_index_in_dim(stored, chosen, 0, keepdims=False)
    return lax.dynamic_update_index_in_dim(stored, jnp.where(active, value, former), chosen, 0)


def body(tokens_in, cotangent, norm_gain, w_gate, w_up, w_down, expert_ids, gate_weights):
    section_count = lax.axis_size("section")
    section_index = lax.axis_index("section")
    device_count = lax.axis_size("expert")
    expert_count = device_count // 2
    micro_count = expert_ids.shape[1]
    tok_rows = expert_ids.shape[2]
    picked = expert_ids.shape[3]
    model_dim = tokens_in.shape[2]
    capacity = 2 * ((tok_rows * picked + expert_count - 1) // expert_count)
    slot_rows = device_count * capacity
    inputs_all, cotangents_all = (
        lax.all_gather(tokens_in, "section", axis=0, tiled=True),
        lax.all_gather(cotangent, "section", axis=0, tiled=True),
    )
    gain_row = norm_gain[0]
    gate_mat = w_gate[0, 0]
    up_mat = w_up[0, 0]
    down_mat = w_down[0, 0]
    hidden_dim = gate_mat.shape[1]
    slot_all, place_all = jax.vmap(
        partial(table_for, expert_count=expert_count, capacity=capacity)
    )(expert_ids[0])
    route_weights = gate_weights[0]

    def dispatch(row_block, place_table):
        packed = jnp.dot(place_table, row_block, preferred_element_type=jnp.float32).astype(
            jnp.bfloat16
        )
        flat_rows = packed.reshape(expert_count, capacity * model_dim)
        doubled = jnp.concatenate([flat_rows, flat_rows], axis=1).reshape(
            device_count, capacity * model_dim
        )
        arrived = lax.all_to_all(doubled, "expert", split_axis=0, concat_axis=0, tiled=True)
        return arrived.reshape(slot_rows, model_dim)

    def collect(partial_out, slot_index):
        flat_rows = partial_out.reshape(device_count, capacity * model_dim)
        returned = lax.all_to_all(flat_rows, "expert", split_axis=0, concat_axis=0, tiled=True)
        paired = returned.reshape(expert_count, 2 * capacity * model_dim).astype(jnp.float32)
        span = capacity * model_dim
        summed = (paired[:, :span] + paired[:, span:]).reshape(expert_count * capacity, model_dim)
        return jnp.take(summed, slot_index, axis=0)

    def forward_expert(row_block):
        gate_pre = jnp.dot(row_block, gate_mat, preferred_element_type=jnp.float32)
        up_pre = jnp.dot(row_block, up_mat, preferred_element_type=jnp.float32)
        hidden = (jax.nn.silu(gate_pre) * up_pre).astype(jnp.bfloat16)
        return (
            jnp.dot(hidden, down_mat, preferred_element_type=jnp.float32).astype(jnp.bfloat16),
            gate_pre,
            up_pre,
        )

    def spare_forward(row_block):
        empty = jnp.zeros((slot_rows, hidden_dim), jnp.float32)
        return (jnp.zeros((slot_rows, model_dim), jnp.bfloat16), empty, empty)

    def backward_expert(operands):
        grad_block, gate_pre, up_pre = operands
        sigma = jax.nn.sigmoid(gate_pre)
        grad_hidden = jnp.dot(grad_block, down_mat.T, preferred_element_type=jnp.float32)
        grad_gate = (grad_hidden * up_pre * sigma * (1.0 + gate_pre * (1.0 - sigma))).astype(
            jnp.bfloat16
        )
        grad_up = (grad_hidden * gate_pre * sigma).astype(jnp.bfloat16)
        total = jnp.dot(grad_gate, gate_mat.T, preferred_element_type=jnp.float32)
        total = total + jnp.dot(grad_up, up_mat.T, preferred_element_type=jnp.float32)
        return total.astype(jnp.bfloat16)

    def spare_backward(operands):
        return jnp.zeros((slot_rows, model_dim), jnp.bfloat16)

    store_in = jnp.zeros((micro_count, tok_rows, model_dim), jnp.bfloat16)
    store_gate = jnp.zeros((micro_count, slot_rows, hidden_dim), jnp.float32)
    store_up = jnp.zeros((micro_count, slot_rows, hidden_dim), jnp.float32)
    store_rows = jnp.zeros((micro_count, tok_rows, picked * model_dim), jnp.float32)
    previous = jnp.zeros((tok_rows, model_dim), jnp.bfloat16)
    for moment in range(micro_count + section_count - 1):
        micro_index = moment - section_index
        active = (micro_index >= 0) & (micro_index < micro_count)
        chosen = jnp.clip(micro_index, 0, micro_count - 1)
        if moment == 0:
            received = previous
        else:
            received = shifted(previous, "section", 1)
        layer_in = jnp.where(section_index == 0, pick_entry(inputs_all, chosen), received)
        values = layer_in.astype(jnp.float32)
        inv_rms = lax.rsqrt(jnp.mean(values * values, axis=-1, keepdims=True) + epsilon)
        normed = (values * inv_rms * gain_row).astype(jnp.bfloat16)
        slot_index = pick_entry(slot_all, chosen)
        arrived = dispatch(jnp.repeat(normed, picked, axis=0), pick_entry(place_all, chosen))
        expert_out, gate_pre, up_pre = lax.cond(active, forward_expert, spare_forward, arrived)
        expert_rows = collect(expert_out, slot_index)
        weights_now = pick_entry(route_weights, chosen)
        mixed = values
        mixed = mixed + weights_now * expert_rows
        previous = mixed.astype(jnp.bfloat16)
        store_in = put_entry(store_in, layer_in, chosen, active)
        store_gate = put_entry(store_gate, gate_pre, chosen, active)
        store_up = put_entry(store_up, up_pre, chosen, active)
        store_rows = put_entry(store_rows, expert_rows, chosen, active)
    grad_out = jnp.zeros((micro_count, tok_rows, model_dim), jnp.bfloat16)
    gate_out = jnp.zeros((micro_count, tok_rows, picked), jnp.float32)
    previous = jnp.zeros((tok_rows, model_dim), jnp.bfloat16)
    for moment in range(micro_count + section_count - 1):
        micro_index = moment - (section_count - 1 - section_index)
        active = (micro_index >= 0) & (micro_index < micro_count)
        chosen = jnp.clip(micro_index, 0, micro_count - 1)
        if moment == 0:
            received = previous
        else:
            received = shifted(previous, "section", -1)
        grad_next = jnp.where(
            section_index == section_count - 1, pick_entry(cotangents_all, chosen), received
        )
        grad_f = grad_next.astype(jnp.float32)
        expert_rows = pick_entry(store_rows, chosen)
        weights_now = pick_entry(route_weights, chosen)
        gate_cols = [jnp.sum(grad_f * expert_rows, axis=-1)]
        grad_cols = weights_now * grad_f
        gate_grad = jnp.stack(gate_cols, axis=1)
        grad_rows = grad_cols.astype(jnp.bfloat16)
        slot_index = pick_entry(slot_all, chosen)
        arrived = dispatch(grad_rows, pick_entry(place_all, chosen))
        grad_part = lax.cond(
            active,
            backward_expert,
            spare_backward,
            (arrived, pick_entry(store_gate, chosen), pick_entry(store_up, chosen)),
        )
        collected = collect(grad_part, slot_index)
        scaled = collected * gain_row
        values = pick_entry(store_in, chosen).astype(jnp.float32)
        inv_rms = lax.rsqrt(jnp.mean(values * values, axis=-1, keepdims=True) + epsilon)
        grad_in = (
            grad_f
            + inv_rms * scaled
            - values
            * (inv_rms * inv_rms * inv_rms)
            * jnp.mean(values * scaled, axis=-1, keepdims=True)
        )
        previous = grad_in.astype(jnp.bfloat16)
        grad_out = put_entry(grad_out, previous, chosen, active)
        gate_out = put_entry(gate_out, gate_grad, chosen, active)
    return (grad_out[None], gate_out[None])


def solution(mesh):
    return jax.shard_map(
        body,
        mesh=mesh,
        in_specs=(
            P("section", "expert", None),
            P("section", "expert", None),
            P("section", None),
            P("section", "expert", None, None),
            P("section", "expert", None, None),
            P("section", "expert", None, None),
            P("section", None, "expert", None),
            P("section", None, "expert", None),
        ),
        out_specs=(P("section", None, "expert", None), P("section", None, "expert", None)),
        check_vma=False,
    )
```

profile of v0, /device:TPU:32, one launch (start us, length us, event | category | flops | bytes accessed | tf_op | source)
XLA Modules:
  0.0 1941.1 jit_solution(15744684650249855149)
XLA Ops:
  3.1 14.4 all_gather.7
  34.2 11.8 all-to-all-start
  45.9 25.2 %all-to-all-done = bf16[64,2,3584]{2,1,0:T(2,128)(2,1)} async-done(((bf16[64,2,3584]{2,1,0:T(2,128)(2,1)}), bf16[64,2,3584]{2,1,0:T(2,128)(2,1)}, u32[]{:S(2)}, u32[]{:S(2)}) %all-to-all-start) | async-done | bytes 917536 | tf_op jit(solution)/shard_map/all_to_all | solution.py:74
  76.5 15.8 conditional.14
  117.1 23.5 %all-to-all-done.1 = bf16[64,2,3584]{2,1,0:T(2,128)(2,1)S(1)} async-done(((bf16[64,2,3584]{2,1,0:T(2,128)(2,1)}), bf16[64,2,3584]{2,1,0:T(2,128)(2,1)S(1)}, u32[]{:S(2)}, u32[]{:S(2)}) %all-to-all-start.1) | async-done | bytes 917536 | tf_op jit(solution)/shard_map/all_to_all | solution.py:79
  188.2 25.2 %all-to-all-done.2 = bf16[64,2,3584]{2,1,0:T(2,128)(2,1)S(1)} async-done(((bf16[64,2,3584]{2,1,0:T(2,128)(2,1)}), bf16[64,2,3584]{2,1,0:T(2,128)(2,1)S(1)}, u32[]{:S(2)}, u32[]{:S(2)}) %all-to-all-start.2) | async-done | bytes 917536 | tf_op jit(solution)/shard_map/all_to_all | solution.py:74
  215.6 16.8 conditional.15
  250.5 25.1 %all-to-all-done.3 = bf16[64,2,3584]{2,1,0:T(2,128)(2,1)S(1)} async-done(((bf16[64,2,3584]{2,1,0:T(2,128)(2,1)}), bf16[64,2,3584]{2,1,0:T(2,128)(2,1)S(1)}, u32[]{:S(2)}, u32[]{:S(2)}) %all-to-all-start.3) | async-done | bytes 917536 | tf_op jit(solution)/shard_map/all_to_all | solution.py:79
  277.6 7.9 convert_reduce_fusion.12
  327.1 25.2 %all-to-all-done.4 = bf16[64,2,3584]{2,1,0:T(2,128)(2,1)S(1)} async-done(((bf16[64,2,3584]{2,1,0:T(2,128)(2,1)}), bf16[64,2,3584]{2,1,0:T(2,128)(2,1)S(1)}, u32[]{:S(2)}, u32[]{:S(2)}) %all-to-all-start.4) | async-done | bytes 917536 | tf_op jit(solution)/shard_map/all_to_all | solution.py:74
  354.5 16.8 conditional.16
  389.4 25.1 %all-to-all-done.5 = bf16[64,2,3584]{2,1,0:T(2,128)(2,1)S(1)} async-done(((bf16[64,2,3584]{2,1,0:T(2,128)(2,1)}), bf16[64,2,3584]{2,1,0:T(2,128)(2,1)S(1)}, u32[]{:S(2)}, u32[]{:S(2)}) %all-to-all-start.5) | async-done | bytes 917536 | tf_op jit(solution)/shard_map/all_to_all | solution.py:79
  466.3 25.1 %all-to-all-done.6 = bf16[64,2,3584]{2,1,0:T(2,128)(2,1)S(1)} async-done(((bf16[64,2,3584]{2,1,0:T(2,128)(2,1)}), bf16[64,2,3584]{2,1,0:T(2,128)(2,1)S(1)}, u32[]{:S(2)}, u32[]{:S(2)}) %all-to-all-start.6) | async-done | bytes 917536 | tf_op jit(solution)/shard_map/all_to_all | solution.py:74
  493.5 16.3 conditional.17
  528.2 25.1 %all-to-all-done.7 = bf16[64,2,3584]{2,1,0:T(2,128)(2,1)S(1)} async-done(((bf16[64,2,3584]{2,1,0:T(2,128)(2,1)}), bf16[64,2,3584]{2,1,0:T(2,128)(2,1)S(1)}, u32[]{:S(2)}, u32[]{:S(2)}) %all-to-all-start.7) | async-done | bytes 917536 | tf_op jit(solution)/shard_map/all_to_all | solution.py:79
  605.0 14.3 all_gather.6
  619.3 10.8 all-to-all-done.8
  644.4 8.1 reduce.52
  679.3 9.2 all-to-all-done.9
  719.7 20.5 %collective-permute-start.4 = (bf16[32,3584]{1,0:T(8,128)(2,1)S(1)}, bf16[32,3584]{1,0:T(8,128)(2,1)S(1)}, u32[]{:S(2)}, u32[]{:S(2)}) collective-permute-start(bf16[32,3584]{1,0:T(8,128)(2,1)S(1)} %fusion.177), channel_id=1, source_target_pairs={{0,64},{64,128},{128,192},{1,65},{65,129},{129,193},{2,66},{66,130... | collective-permute-start | bytes 688136 | tf_op jit(solution)/shard_map/ppermute | solution.py:14
  759.4 10.3 all-to-all-start.10
  780.0 14.9 all-to-all-done.10
  797.0 8.7 conditional.19
  836.9 15.1 all-to-all-done.11
  911.5 16.5 all-to-all-done.13
  935.5 8.8 conditional.21
  962.2 25.1 %all-to-all-done.14 = bf16[64,2,3584]{2,1,0:T(2,128)(2,1)S(1)} async-done(((bf16[64,2,3584]{2,1,0:T(2,128)(2,1)}), bf16[64,2,3584]{2,1,0:T(2,128)(2,1)S(1)}, u32[]{:S(2)}, u32[]{:S(2)}) %all-to-all-start.14) | async-done | bytes 917536 | tf_op jit(solution)/shard_map/all_to_all | solution.py:79
  1009.2 15.5 collective-permute-done.6
  1034.8 8.1 reduce.58
  1053.5 25.2 %all-to-all-done.15 = bf16[64,2,3584]{2,1,0:T(2,128)(2,1)} async-done(((bf16[64,2,3584]{2,1,0:T(2,128)(2,1)}), bf16[64,2,3584]{2,1,0:T(2,128)(2,1)}, u32[]{:S(2)}, u32[]{:S(2)}) %all-to-all-start.15) | async-done | bytes 917536 | tf_op jit(solution)/shard_map/all_to_all | solution.py:74
  1098.2 8.1 reduce.59
  1117.9 24.2 %all-to-all-done.16 = bf16[64,2,3584]{2,1,0:T(2,128)(2,1)} async-done(((bf16[64,2,3584]{2,1,0:T(2,128)(2,1)}), bf16[64,2,3584]{2,1,0:T(2,128)(2,1)}, u32[]{:S(2)}, u32[]{:S(2)}) %all-to-all-start.16) | async-done | bytes 917536 | tf_op jit(solution)/shard_map/all_to_all | solution.py:79
  1169.7 8.5 collective-permute-done.7
  1200.6 25.2 %all-to-all-done.17 = bf16[64,2,3584]{2,1,0:T(2,128)(2,1)S(1)} async-done(((bf16[64,2,3584]{2,1,0:T(2,128)(2,1)}), bf16[64,2,3584]{2,1,0:T(2,128)(2,1)S(1)}, u32[]{:S(2)}, u32[]{:S(2)}) %all-to-all-start.17) | async-done | bytes 917536 | tf_op jit(solution)/shard_map/all_to_all | solution.py:74
  1253.4 23.4 %all-to-all-done.18 = bf16[64,2,3584]{2,1,0:T(2,128)(2,1)S(1)} async-done(((bf16[64,2,3584]{2,1,0:T(2,128)(2,1)}), bf16[64,2,3584]{2,1,0:T(2,128)(2,1)S(1)}, u32[]{:S(2)}, u32[]{:S(2)}) %all-to-all-start.18) | async-done | bytes 917536 | tf_op jit(solution)/shard_map/all_to_all | solution.py:79
  1300.1 50.5 %collective-permute-done.8 = bf16[32,3584]{1,0:T(8,128)(2,1)S(1)} collective-permute-done((bf16[32,3584]{1,0:T(8,128)(2,1)S(1)}, bf16[32,3584]{1,0:T(8,128)(2,1)S(1)}, u32[]{:S(2)}, u32[]{:S(2)}) %collective-permute-start.8) | collective-permute-done | bytes 229408 | tf_op jit(solution)/shard_map/ppermute | solution.py:14
  1373.7 25.0 %all-to-all-done.19 = bf16[64,2,3584]{2,1,0:T(2,128)(2,1)S(1)} async-done(((bf16[64,2,3584]{2,1,0:T(2,128)(2,1)}), bf16[64,2,3584]{2,1,0:T(2,128)(2,1)S(1)}, u32[]{:S(2)}, u32[]{:S(2)}) %all-to-all-start.19) | async-done | bytes 917536 | tf_op jit(solution)/shard_map/all_to_all | solution.py:74
  1400.8 16.2 conditional.24
  1441.2 19.1 all-to-all-done.20
  1522.8 21.3 %all-to-all-done.21 = bf16[64,2,3584]{2,1,0:T(2,128)(2,1)} async-done(((bf16[64,2,3584]{2,1,0:T(2,128)(2,1)}), bf16[64,2,3584]{2,1,0:T(2,128)(2,1)}, u32[]{:S(2)}, u32[]{:S(2)}) %all-to-all-start.21) | async-done | bytes 917536 | tf_op jit(solution)/shard_map/all_to_all | solution.py:74
  1550.5 16.4 conditional.25
  1590.2 19.6 %all-to-all-done.22 = bf16[64,2,3584]{2,1,0:T(2,128)(2,1)S(1)} async-done(((bf16[64,2,3584]{2,1,0:T(2,128)(2,1)}), bf16[64,2,3584]{2,1,0:T(2,128)(2,1)S(1)}, u32[]{:S(2)}, u32[]{:S(2)}) %all-to-all-start.22) | async-done | bytes 917536 | tf_op jit(solution)/shard_map/all_to_all | solution.py:79
  1667.6 11.3 all-to-all-done.27
  1717.4 16.7 conditional.26
  1759.4 17.9 all-to-all-done.24
  1834.1 25.2 %all-to-all-done.25 = bf16[64,2,3584]{2,1,0:T(2,128)(2,1)S(1)} async-done(((bf16[64,2,3584]{2,1,0:T(2,128)(2,1)}), bf16[64,2,3584]{2,1,0:T(2,128)(2,1)S(1)}, u32[]{:S(2)}, u32[]{:S(2)}) %all-to-all-start.25) | async-done | bytes 917536 | tf_op jit(solution)/shard_map/all_to_all | solution.py:74
  1861.5 16.7 conditional.27
  1897.1 23.8 %all-to-all-done.26 = bf16[64,2,3584]{2,1,0:T(2,128)(2,1)S(1)} async-done(((bf16[64,2,3584]{2,1,0:T(2,128)(2,1)}), bf16[64,2,3584]{2,1,0:T(2,128)(2,1)S(1)}, u32[]{:S(2)}, u32[]{:S(2)}) %all-to-all-start.26) | async-done | bytes 917536 | tf_op jit(solution)/shard_map/all_to_all | solution.py:79
  (628 shorter events, 1195.8 us)
Async XLA Ops:
  17.5 727.6 %copy-start.28 = (bf16[4,32,3584]{2,1,0:T(8,128)(2,1)}, bf16[4,32,3584]{2,1,0:T(8,128)(2,1)S(1)}, u32[]{:S(2)}) copy-start(bf16[4,32,3584]{2,1,0:T(8,128)(2,1)S(1)} %all_gather.7) | copy-start | bytes 2752516
  34.2 36.9 %all-to-all-start = ((bf16[64,2,3584]{2,1,0:T(2,128)(2,1)}), bf16[64,2,3584]{2,1,0:T(2,128)(2,1)}, u32[]{:S(2)}, u32[]{:S(2)}) async-start(bf16[64,2,3584]{2,1,0:T(2,128)(2,1)} %reshape.918), calls=%async_computation | async-start | bytes 1835008 | tf_op jit(solution)/shard_map/all_to_all | solution.py:74
  108.2 32.4 %all-to-all-start.1 = ((bf16[64,2,3584]{2,1,0:T(2,128)(2,1)}), bf16[64,2,3584]{2,1,0:T(2,128)(2,1)S(1)}, u32[]{:S(2)}, u32[]{:S(2)}) async-start(bf16[64,2,3584]{2,1,0:T(2,128)(2,1)} %reshape.920), calls=%async_computation.1 | async-start | bytes 1835008 | tf_op jit(solution)/shard_map/all_to_all | solution.py:79
  116.3 41.9 %copy-start.67 = (pred[32]{0:T(512)(128)(4,1)}, pred[32]{0:T(512)(128)(4,1)S(1)}, u32[]{:S(2)}) copy-start(pred[32]{0:T(512)(128)(4,1)S(1)} %get-tuple-element.838) | copy-start | bytes 100
  116.3 176.8 %copy-start.74 = (pred[32]{0:T(512)(128)(4,1)}, pred[32]{0:T(512)(128)(4,1)S(1)}, u32[]{:S(2)}) copy-start(pred[32]{0:T(512)(128)(4,1)S(1)} %get-tuple-element.836) | copy-start | bytes 100
  116.3 315.7 %copy-start.72 = (pred[32]{0:T(512)(128)(4,1)}, pred[32]{0:T(512)(128)(4,1)S(1)}, u32[]{:S(2)}) copy-start(pred[32]{0:T(512)(128)(4,1)S(1)} %get-tuple-element.834) | copy-start | bytes 100
  158.3 6.5 collective-permute-start
  181.4 32.0 %all-to-all-start.2 = ((bf16[64,2,3584]{2,1,0:T(2,128)(2,1)}), bf16[64,2,3584]{2,1,0:T(2,128)(2,1)S(1)}, u32[]{:S(2)}, u32[]{:S(2)}) async-start(bf16[64,2,3584]{2,1,0:T(2,128)(2,1)} %reshape.922), calls=%async_computation.2 | async-start | bytes 1835008 | tf_op jit(solution)/shard_map/all_to_all | solution.py:74
  243.1 32.4 %all-to-all-start.3 = ((bf16[64,2,3584]{2,1,0:T(2,128)(2,1)}), bf16[64,2,3584]{2,1,0:T(2,128)(2,1)S(1)}, u32[]{:S(2)}, u32[]{:S(2)}) async-start(bf16[64,2,3584]{2,1,0:T(2,128)(2,1)} %reshape.924), calls=%async_computation.3 | async-start | bytes 1835008 | tf_op jit(solution)/shard_map/all_to_all | solution.py:79
  294.4 9.3 collective-permute-start.1
  320.3 32.0 %all-to-all-start.4 = ((bf16[64,2,3584]{2,1,0:T(2,128)(2,1)}), bf16[64,2,3584]{2,1,0:T(2,128)(2,1)S(1)}, u32[]{:S(2)}, u32[]{:S(2)}) async-start(bf16[64,2,3584]{2,1,0:T(2,128)(2,1)} %reshape.926), calls=%async_computation.4 | async-start | bytes 1835008 | tf_op jit(solution)/shard_map/all_to_all | solution.py:74
  382.0 32.4 %all-to-all-start.5 = ((bf16[64,2,3584]{2,1,0:T(2,128)(2,1)}), bf16[64,2,3584]{2,1,0:T(2,128)(2,1)S(1)}, u32[]{:S(2)}, u32[]{:S(2)}) async-start(bf16[64,2,3584]{2,1,0:T(2,128)(2,1)} %reshape.928), calls=%async_computation.5 | async-start | bytes 1835008 | tf_op jit(solution)/shard_map/all_to_all | solution.py:79
  433.3 9.3 collective-permute-start.2
  459.2 32.2 %all-to-all-start.6 = ((bf16[64,2,3584]{2,1,0:T(2,128)(2,1)}), bf16[64,2,3584]{2,1,0:T(2,128)(2,1)S(1)}, u32[]{:S(2)}, u32[]{:S(2)}) async-start(bf16[64,2,3584]{2,1,0:T(2,128)(2,1)} %reshape.930), calls=%async_computation.6 | async-start | bytes 1835008 | tf_op jit(solution)/shard_map/all_to_all | solution.py:74
  520.9 32.4 %all-to-all-start.7 = ((bf16[64,2,3584]{2,1,0:T(2,128)(2,1)}), bf16[64,2,3584]{2,1,0:T(2,128)(2,1)S(1)}, u32[]{:S(2)}, u32[]{:S(2)}) async-start(bf16[64,2,3584]{2,1,0:T(2,128)(2,1)} %reshape.932), calls=%async_computation.7 | async-start | bytes 1835008 | tf_op jit(solution)/shard_map/all_to_all | solution.py:79
  571.9 9.3 collective-permute-start.3
  598.0 32.1 %all-to-all-start.8 = ((bf16[64,2,3584]{2,1,0:T(2,128)(2,1)}), bf16[64,2,3584]{2,1,0:T(2,128)(2,1)}, u32[]{:S(2)}, u32[]{:S(2)}) async-start(bf16[64,2,3584]{2,1,0:T(2,128)(2,1)} %reshape.934), calls=%async_computation.8 | async-start | bytes 1835008 | tf_op jit(solution)/shard_map/all_to_all | solution.py:74
  619.3 44.2 %copy-start.31 = (bf16[4,32,3584]{2,1,0:T(8,128)(2,1)}, bf16[4,32,3584]{2,1,0:T(8,128)(2,1)S(1)}, u32[]{:S(2)}) copy-start(bf16[4,32,3584]{2,1,0:T(8,128)(2,1)S(1)} %all_gather.6) | copy-start | bytes 2752516
  656.1 32.5 %all-to-all-start.9 = ((bf16[64,2,3584]{2,1,0:T(2,128)(2,1)}), bf16[64,2,3584]{2,1,0:T(2,128)(2,1)}, u32[]{:S(2)}, u32[]{:S(2)}) async-start(bf16[64,2,3584]{2,1,0:T(2,128)(2,1)} %reshape.936), calls=%async_computation.9 | async-start | bytes 1835008 | tf_op jit(solution)/shard_map/all_to_all | solution.py:79
  688.5 70.9 %all-to-all-start.12 = ((bf16[64,2,3584]{2,1,0:T(2,128)(2,1)}), bf16[64,2,3584]{2,1,0:T(2,128)(2,1)}, u32[]{:S(2)}, u32[]{:S(2)}) async-start(bf16[64,2,3584]{2,1,0:T(2,128)(2,1)} %reshape.916), calls=%async_computation.12 | async-start | bytes 1835008 | tf_op jit(solution)/shard_map/all_to_all | solution.py:74
  719.7 25.4 %collective-permute-start.4 = (bf16[32,3584]{1,0:T(8,128)(2,1)S(1)}, bf16[32,3584]{1,0:T(8,128)(2,1)S(1)}, u32[]{:S(2)}, u32[]{:S(2)}) collective-permute-start(bf16[32,3584]{1,0:T(8,128)(2,1)S(1)} %fusion.177), channel_id=1, source_target_pairs={{0,64},{64,128},{128,192},{1,65},{65,129},{129,193},{2,66},{66,130... | collective-permute-start | bytes 688136 | tf_op jit(solution)/shard_map/ppermute | solution.py:14
  759.4 35.6 %all-to-all-start.10 = ((bf16[64,2,3584]{2,1,0:T(2,128)(2,1)}), bf16[64,2,3584]{2,1,0:T(2,128)(2,1)S(1)}, u32[]{:S(2)}, u32[]{:S(2)}) async-start(bf16[64,2,3584]{2,1,0:T(2,128)(2,1)} %reshape.938), calls=%async_computation.10 | async-start | bytes 1835008 | tf_op jit(solution)/shard_map/all_to_all | solution.py:74
  819.8 32.1 %all-to-all-start.11 = ((bf16[64,2,3584]{2,1,0:T(2,128)(2,1)}), bf16[64,2,3584]{2,1,0:T(2,128)(2,1)S(1)}, u32[]{:S(2)}, u32[]{:S(2)}) async-start(bf16[64,2,3584]{2,1,0:T(2,128)(2,1)} %reshape.940), calls=%async_computation.11 | async-start | bytes 1835008 | tf_op jit(solution)/shard_map/all_to_all | solution.py:79
  871.6 9.3 collective-permute-start.5
  896.0 32.0 %all-to-all-start.13 = ((bf16[64,2,3584]{2,1,0:T(2,128)(2,1)}), bf16[64,2,3584]{2,1,0:T(2,128)(2,1)S(1)}, u32[]{:S(2)}, u32[]{:S(2)}) async-start(bf16[64,2,3584]{2,1,0:T(2,128)(2,1)} %reshape.942), calls=%async_computation.13 | async-start | bytes 1835008 | tf_op jit(solution)/shard_map/all_to_all | solution.py:74
  955.1 32.2 %all-to-all-start.14 = ((bf16[64,2,3584]{2,1,0:T(2,128)(2,1)}), bf16[64,2,3584]{2,1,0:T(2,128)(2,1)S(1)}, u32[]{:S(2)}, u32[]{:S(2)}) async-start(bf16[64,2,3584]{2,1,0:T(2,128)(2,1)} %reshape.944), calls=%async_computation.14 | async-start | bytes 1835008 | tf_op jit(solution)/shard_map/all_to_all | solution.py:79
  1007.7 109.5 %copy-start.29 = (bf16[4,32,3584]{2,1,0:T(8,128)(2,1)}, bf16[4,32,3584]{2,1,0:T(8,128)(2,1)S(1)}, u32[]{:S(2)}) copy-start(bf16[4,32,3584]{2,1,0:T(8,128)(2,1)S(1)} %get-tuple-element.786) | copy-start | bytes 2752516
  1007.7 17.1 collective-permute-start.6
  1046.5 32.1 %all-to-all-start.15 = ((bf16[64,2,3584]{2,1,0:T(2,128)(2,1)}), bf16[64,2,3584]{2,1,0:T(2,128)(2,1)}, u32[]{:S(2)}, u32[]{:S(2)}) async-start(bf16[64,2,3584]{2,1,0:T(2,128)(2,1)} %reshape.946), calls=%async_computation.15 | async-start | bytes 1835008 | tf_op jit(solution)/shard_map/all_to_all | solution.py:74
  1109.8 32.3 %all-to-all-start.16 = ((bf16[64,2,3584]{2,1,0:T(2,128)(2,1)}), bf16[64,2,3584]{2,1,0:T(2,128)(2,1)}, u32[]{:S(2)}, u32[]{:S(2)}) async-start(bf16[64,2,3584]{2,1,0:T(2,128)(2,1)} %reshape.948), calls=%async_computation.16 | async-start | bytes 1835008 | tf_op jit(solution)/shard_map/all_to_all | solution.py:79
  1168.1 10.0 collective-permute-start.7
  1193.7 32.0 %all-to-all-start.17 = ((bf16[64,2,3584]{2,1,0:T(2,128)(2,1)}), bf16[64,2,3584]{2,1,0:T(2,128)(2,1)S(1)}, u32[]{:S(2)}, u32[]{:S(2)}) async-start(bf16[64,2,3584]{2,1,0:T(2,128)(2,1)} %reshape.950), calls=%async_computation.17 | async-start | bytes 1835008 | tf_op jit(solution)/shard_map/all_to_all | solution.py:74
  1244.6 32.2 %all-to-all-start.18 = ((bf16[64,2,3584]{2,1,0:T(2,128)(2,1)}), bf16[64,2,3584]{2,1,0:T(2,128)(2,1)S(1)}, u32[]{:S(2)}, u32[]{:S(2)}) async-start(bf16[64,2,3584]{2,1,0:T(2,128)(2,1)} %reshape.952), calls=%async_computation.18 | async-start | bytes 1835008 | tf_op jit(solution)/shard_map/all_to_all | solution.py:79
  1295.1 57.1 %copy-start.89 = (f32[32]{0:T(128)S(1)}, f32[32]{0:T(128)}, u32[]{:S(2)}) copy-start(f32[32]{0:T(128)} %get-tuple-element.842) | copy-start | bytes 388
  1298.5 52.0 %collective-permute-start.8 = (bf16[32,3584]{1,0:T(8,128)(2,1)S(1)}, bf16[32,3584]{1,0:T(8,128)(2,1)S(1)}, u32[]{:S(2)}, u32[]{:S(2)}) collective-permute-start(bf16[32,3584]{1,0:T(8,128)(2,1)S(1)} %get-tuple-element.779), channel_id=1, source_target_pairs={{64,0},{128,64},{192,128},{65,1},{129,65},{193,129},{66,2},{130,66... | collective-permute-start | bytes 688136 | tf_op jit(solution)/shard_map/ppermute | solution.py:14
  1366.2 32.5 %all-to-all-start.19 = ((bf16[64,2,3584]{2,1,0:T(2,128)(2,1)}), bf16[64,2,3584]{2,1,0:T(2,128)(2,1)S(1)}, u32[]{:S(2)}, u32[]{:S(2)}) async-start(bf16[64,2,3584]{2,1,0:T(2,128)(2,1)} %reshape.954), calls=%async_computation.19 | async-start | bytes 1835008 | tf_op jit(solution)/shard_map/all_to_all | solution.py:74
  1428.0 32.4 %all-to-all-start.20 = ((bf16[64,2,3584]{2,1,0:T(2,128)(2,1)}), bf16[64,2,3584]{2,1,0:T(2,128)(2,1)}, u32[]{:S(2)}, u32[]{:S(2)}) async-start(bf16[64,2,3584]{2,1,0:T(2,128)(2,1)} %reshape.956), calls=%async_computation.20 | async-start | bytes 1835008 | tf_op jit(solution)/shard_map/all_to_all | solution.py:79
  1486.5 9.3 collective-permute-start.9
  1511.9 32.3 %all-to-all-start.21 = ((bf16[64,2,3584]{2,1,0:T(2,128)(2,1)}), bf16[64,2,3584]{2,1,0:T(2,128)(2,1)}, u32[]{:S(2)}, u32[]{:S(2)}) async-start(bf16[64,2,3584]{2,1,0:T(2,128)(2,1)} %reshape.958), calls=%async_computation.21 | async-start | bytes 1835008 | tf_op jit(solution)/shard_map/all_to_all | solution.py:74
  1577.7 32.1 %all-to-all-start.22 = ((bf16[64,2,3584]{2,1,0:T(2,128)(2,1)}), bf16[64,2,3584]{2,1,0:T(2,128)(2,1)S(1)}, u32[]{:S(2)}, u32[]{:S(2)}) async-start(bf16[64,2,3584]{2,1,0:T(2,128)(2,1)} %reshape.960), calls=%async_computation.22 | async-start | bytes 1835008 | tf_op jit(solution)/shard_map/all_to_all | solution.py:79
  1629.8 24.1 %collective-permute-start.10 = (bf16[32,3584]{1,0:T(8,128)(2,1)}, bf16[32,3584]{1,0:T(8,128)(2,1)S(1)}, u32[]{:S(2)}, u32[]{:S(2)}) collective-permute-start(bf16[32,3584]{1,0:T(8,128)(2,1)} %get-tuple-element.771), channel_id=1, source_target_pairs={{64,0},{128,64},{192,128},{65,1},{129,65},{193,129},{66,2},{130,66... | collective-permute-start | bytes 688136 | tf_op jit(solution)/shard_map/ppermute | solution.py:14
  1646.3 32.5 %all-to-all-start.27 = ((bf16[64,2,3584]{2,1,0:T(2,128)(2,1)}), bf16[64,2,3584]{2,1,0:T(2,128)(2,1)}, u32[]{:S(2)}, u32[]{:S(2)}) async-start(bf16[64,2,3584]{2,1,0:T(2,128)(2,1)} %reshape.970), calls=%async_computation.27 | async-start | bytes 1835008 | tf_op jit(solution)/shard_map/all_to_all | solution.py:79
  1678.8 32.2 %all-to-all-start.23 = ((bf16[64,2,3584]{2,1,0:T(2,128)(2,1)}), bf16[64,2,3584]{2,1,0:T(2,128)(2,1)}, u32[]{:S(2)}, u32[]{:S(2)}) async-start(bf16[64,2,3584]{2,1,0:T(2,128)(2,1)} %reshape.962), calls=%async_computation.23 | async-start | bytes 1835008 | tf_op jit(solution)/shard_map/all_to_all | solution.py:74
  1744.8 32.5 %all-to-all-start.24 = ((bf16[64,2,3584]{2,1,0:T(2,128)(2,1)}), bf16[64,2,3584]{2,1,0:T(2,128)(2,1)}, u32[]{:S(2)}, u32[]{:S(2)}) async-start(bf16[64,2,3584]{2,1,0:T(2,128)(2,1)} %reshape.964), calls=%async_computation.24 | async-start | bytes 1835008 | tf_op jit(solution)/shard_map/all_to_all | solution.py:79
  1801.8 10.2 collective-permute-start.11
  1827.3 32.0 %all-to-all-start.25 = ((bf16[64,2,3584]{2,1,0:T(2,128)(2,1)}), bf16[64,2,3584]{2,1,0:T(2,128)(2,1)S(1)}, u32[]{:S(2)}, u32[]{:S(2)}) async-start(bf16[64,2,3584]{2,1,0:T(2,128)(2,1)} %reshape.966), calls=%async_computation.25 | async-start | bytes 1835008 | tf_op jit(solution)/shard_map/all_to_all | solution.py:74
  1889.0 32.0 %all-to-all-start.26 = ((bf16[64,2,3584]{2,1,0:T(2,128)(2,1)}), bf16[64,2,3584]{2,1,0:T(2,128)(2,1)S(1)}, u32[]{:S(2)}, u32[]{:S(2)}) async-start(bf16[64,2,3584]{2,1,0:T(2,128)(2,1)} %reshape.968), calls=%async_computation.26 | async-start | bytes 1835008 | tf_op jit(solution)/shard_map/all_to_all | solution.py:79
  1897.1 33.8 %copy-start.66 = (f32[1,4,32,1]{2,1,3,0:T(4,128)}, f32[1,4,32,1]{2,1,3,0:T(4,128)S(1)}, u32[]{:S(2)}) copy-start(f32[1,4,32,1]{2,1,3,0:T(4,128)S(1)} %dynamic_update_slice.173) | copy-start | bytes 1540
  (70 other events, 401.9 us)
where the time goes:
time: 1960 us; the launch traced here: 1940 us
  waiting for transfers between devices  674 us (34%)
  other arithmetic  489 us (25%)
  local copies, waits for them, and re-layouts  396 us (20%)
  starting transfers between devices  257 us (13%)
  matrix products  61.6 us (3%)
  loops' own time  31.1 us (2%)
  blocking collectives  28.8 us (1%)
    all_to_all x14, waiting for transfers between devices, collect(): lax.all_to_all(flat_rows, 'expert', split_axis=0, concat_axis=0, tiled=True)  287 us
    all_to_all x14, waiting for transfers between devices, dispatch(): lax.all_to_all(doubled, 'expert', split_axis=0, concat_axis=0, tiled=True)  269 us
    unnamed x181, local copies, waits for them, and re-layouts  165 us
    ppermute x12, waiting for transfers between devices, shifted(): return lax.ppermute(block, axis, route)  118 us
    convert_element_type x14, other arithmetic, collect(): returned.reshape(expert_count, 2 * capacity * model_dim).astype(jnp.float32)  111 us
    all_to_all x14, starting transfers between devices, dispatch(): lax.all_to_all(doubled, 'expert', split_axis=0, concat_axis=0, tiled=True)  106 us
    all_to_all x14, other arithmetic, collect(): lax.all_to_all(flat_rows, 'expert', split_axis=0, concat_axis=0, tiled=True)  102 us
    all_to_all x14, starting transfers between devices, collect(): lax.all_to_all(flat_rows, 'expert', split_axis=0, concat_axis=0, tiled=True)  102 us
  transfers between devices with their start and end apart: 40, of which 38 were waited for; matrix products, arithmetic and copies ran while one was open for 8% of the time, Pallas kernels for 0%

commit v1 on v0

v1 whole, which is shorter than its diff:
```python
import functools

import jax
import jax.numpy as jnp
from jax import lax
from jax.experimental import pallas as pl
from jax.experimental.pallas import tpu as pltpu
from jax.sharding import PartitionSpec as P

MESH = pl.DeviceIdType.MESH
EPS = 1e-06
MICRO = 4
TOK = 32
CHIPS = 32
WIDTH = 3584
HALF = 512
ROWS = 2 * CHIPS
LANES = (512, 384)
STARTS = (0, 2048)
PARTS = len(LANES)
F32 = jnp.float32
BF16 = jnp.bfloat16
NT = (((1,), (1,)), ((), ()))
TILE = 256


def iota(shape, dim):
    return lax.broadcasted_iota(jnp.int32, shape, dim)


def kernel(
    tok_ref, cot_ref, gain_ref, wg_ref, wu_ref, wd_ref, idrow_ref, idcol_ref, gate_ref,
    gin_ref, ggate_ref,
    wg, wu, wd, place, pick, back,
    hbuf, gbuf, disp_f, disp_b, coll_f, coll_b, send_df, send_db, send_cf, send_cb,
    hsend, gsend, erows, hrows, gate_pre, up_pre, rms_all, acc_a, acc_b, act,
    w_send, w_recv, w_local, h_recv, g_recv, h_ssem, g_ssem,
    df_r, db_r, cf_r, cb_r, df_s, db_s, cf_s, cb_s,
):
    s, me = lax.axis_index("section"), lax.axis_index("expert")
    chip, core = me // 2, me % 2
    cx, cz = chip // 8, chip % 8
    sibling = me + 1 - 2 * core

    def peer(i):
        return (((cx + i // 8) % 4) * 8 + (cz + i % 8) % 8) * 2 + core

    local = []
    for n, (src, dst) in enumerate(((wg_ref, wg), (wu_ref, wu), (wd_ref, wd))):
        local.append(pltpu.make_async_copy(src.at[0, 0], dst.at[core], w_local.at[n]))
        local[-1].start()

    barrier = pltpu.get_barrier_semaphore()

    def greet(i, carry):
        pl.semaphore_signal(barrier, inc=1, device_id=(s, peer(i)), device_id_type=MESH)
        return carry

    lax.fori_loop(1, CHIPS, greet, 0)
    pl.semaphore_signal(barrier, inc=1, device_id=(s, sibling), device_id_type=MESH)
    for i in range(1, 4):
        pl.semaphore_signal(barrier, inc=1, device_id=((s + i) % 4, me), device_id_type=MESH)
    pl.semaphore_wait(barrier, CHIPS + 3)

    shared = []
    for n, (src, dst) in enumerate(((wg_ref, wg), (wu_ref, wu), (wd_ref, wd))):
        shared.append(
            pltpu.make_async_remote_copy(
                src.at[0, 0], dst.at[core], w_send.at[n], w_recv.at[n],
                device_id=(s, sibling), device_id_type=MESH,
            )
        )
        shared[-1].start()

    def stack(src, dst, p):
        w = LANES[p]
        for q in range(4):
            cols = slice(STARTS[p] + q * w, STARTS[p] + (q + 1) * w)
            dst[q * TOK : (q + 1) * TOK, :] = src[0, :, cols]

    def bring(src, stage, held, ssem, recv, p, owner):
        @pl.when(s == owner)
        def _():
            stack(src, held[p].at[owner], p)

        @pl.when(s != owner)
        def _():
            stack(src, stage[p], p)
            pltpu.make_async_remote_copy(
                stage[p], held[p].at[s], ssem.at[p], recv[p].at[s],
                device_id=(owner, me), device_id_type=MESH,
            ).start()

    for p in range(PARTS):
        bring(tok_ref, hsend, hbuf, h_ssem, h_recv, p, 0)
        bring(cot_ref, gsend, gbuf, g_ssem, g_recv, p, 3)

    def tables(m, carry):
        idrow, idcol = idrow_ref[m], idcol_ref[m]
        same = idcol == idrow
        ti, tj = iota((128, 128), 0), iota((128, 128), 1)
        before_row = same & (ti < TOK) & (ti < tj % TOK)
        before_col = same & (tj < TOK) & (tj < ti % TOK)
        slot_row = 2 * idrow + jnp.sum(before_row.astype(jnp.int32), axis=0, keepdims=True)
        slot_col = 2 * idcol + jnp.sum(before_col.astype(jnp.int32), axis=1, keepdims=True)
        r, c = iota((256, 128), 0), iota((256, 128), 1)
        hit = ((r // 8) * 2 + r % 2 == slot_row) & ((r // 2) % 4 == c // TOK)
        place[m] = hit.astype(F32).astype(BF16)
        r, c = iota((128, 256), 1), iota((128, 256), 0)
        hit = ((r // 8) * 2 + r % 2 == slot_col) & ((r // 2) % 4 == c // TOK)
        pick[m] = hit.astype(F32).astype(BF16)
        return carry

    lax.fori_loop(0, MICRO, tables, 0)
    r, c = iota((256, 256), 0), iota((256, 256), 1)
    back[0] = (c == ((r // 2) % 32) * 8 + (r // 64) * 2 + r % 2).astype(F32).astype(BF16)
    back[1] = (r == ((c // 2) % 32) * 8 + (c // 64) * 2 + c % 2).astype(F32).astype(BF16)

    def wait_all(ref, sem):
        pltpu.make_async_copy(ref, ref, sem).wait()

    def scatter(src, dst, m, ssem, rsem):
        def one(i, carry):
            t = peer(i)
            pltpu.make_async_remote_copy(
                src.at[t // 2], dst.at[m, chip], ssem, rsem, device_id=(s, t), device_id_type=MESH
            ).start()
            return carry

        pltpu.make_async_copy(src.at[chip], dst.at[m, chip], rsem).start()
        lax.fori_loop(1, CHIPS, one, 0)

    def sent(src, ssem):
        wait_all(src.at[pl.ds(0, CHIPS - 1)], ssem)

    def put(dst, value, w):
        dst[...] = value.reshape(CHIPS, 8, w).astype(BF16)

    def chunks(ref, m, w):
        return ref[m].astype(F32).reshape(256, w).astype(BF16)

    def dot(a, b):
        return jnp.dot(a, b, preferred_element_type=F32)

    def dispatch_forward(m):
        for p in range(PARTS):
            @pl.when((s != 0) | (m != 0))
            def _():
                wait_all(hbuf[p].at[m], h_recv[p].at[m])

            @pl.when(m > 0)
            def _():
                sent(send_df[p], df_s.at[p])

            put(send_df[p], dot(place[m], hbuf[p][m]), LANES[p])
            scatter(send_df[p], disp_f[p], m, df_s.at[p], df_r[p].at[m])

    def expert_forward(m):
        total = jnp.zeros((ROWS, 1), F32)
        for p in range(PARTS):
            w = LANES[p]
            wait_all(disp_f[p].at[m], df_r[p].at[m])
            rows = dot(back[0], chunks(disp_f[p], m, w))
            for q in range(4):
                block = rows[q * ROWS : (q + 1) * ROWS]
                total = total + jnp.sum(block * block, axis=1, keepdims=True)
                cols = slice(STARTS[p] + q * w, STARTS[p] + (q + 1) * w)
                hrows[m, :, cols] = block.astype(BF16)
                act[:, cols] = (block * gain_ref[0:1, cols]).astype(BF16)
            if p == 0:
                @pl.when(m == 0)
                def _():
                    for n in range(2):
                        local[n].wait()
                        shared[n].wait_recv()
            feats = slice(STARTS[p], STARTS[p] + 4 * w)

            def tile(i, carry):
                hf, at = i // 2, pl.ds(pl.multiple_of((i % 2) * TILE, TILE), TILE)
                to = pl.ds(pl.multiple_of(i * TILE, TILE), TILE)
                x = act[:, feats]
                a, b = dot(x, wg[hf, feats, at]), dot(x, wu[hf, feats, at])
                if p > 0:
                    a, b = a + acc_a[:, to], b + acc_b[:, to]
                acc_a[:, to] = a
                acc_b[:, to] = b
                return carry

            lax.fori_loop(0, 4, tile, 0)
        inv = lax.rsqrt(total * (1.0 / WIDTH) + EPS)
        rms_all[m] = jnp.broadcast_to(inv, (ROWS, 128))
        a, b = acc_a[...] * inv, acc_b[...] * inv
        gate_pre[m] = a
        up_pre[m] = b
        act[:, : 2 * HALF] = (a * jax.nn.sigmoid(a) * b).astype(BF16)

        @pl.when(m == 0)
        def _():
            local[2].wait()
            shared[2].wait_recv()

        for p in range(PARTS):
            w = LANES[p]
            blocks = []
            for q in range(4):
                cols = slice(STARTS[p] + q * w, STARTS[p] + (q + 1) * w)
                y = dot(act[:, :HALF], wd[0, :, cols]) + dot(act[:, HALF : 2 * HALF], wd[1, :, cols])
                blocks.append(y.astype(BF16))

            @pl.when(m > 0)
            def _():
                sent(send_cf[p], cf_s.at[p])

            put(send_cf[p], dot(back[1], jnp.concatenate(blocks, axis=0)), w)
            scatter(send_cf[p], coll_f[p], m, cf_s.at[p], cf_r[p].at[m])

    def combine_forward(m):
        for p in range(PARTS):
            w = LANES[p]
            wait_all(coll_f[p].at[m], cf_r[p].at[m])
            rows = dot(pick[m], chunks(coll_f[p], m, w))
            erows[p][m] = rows.astype(BF16)

            @pl.when(s < 3)
            def _():
                @pl.when((m > 0) | (s != 0))
                def _():
                    wait_all(hsend[p], h_ssem.at[p])

                hsend[p][...] = (hbuf[p][m].astype(F32) + gate_ref[m] * rows).astype(BF16)
                pltpu.make_async_remote_copy(
                    hsend[p], hbuf[p].at[m], h_ssem.at[p], h_recv[p].at[m],
                    device_id=(s + 1, me), device_id_type=MESH,
                ).start()

    def dispatch_backward(m):
        for p in range(PARTS):
            @pl.when((s != 3) | (m != 3))
            def _():
                wait_all(gbuf[p].at[m], g_recv[p].at[m])

            @pl.when(m > 0)
            def _():
                sent(send_db[p], db_s.at[p])

            grads = (gate_ref[m] * gbuf[p][m].astype(F32)).astype(BF16)
            put(send_db[p], dot(place[m], grads), LANES[p])
            scatter(send_db[p], disp_b[p], m, db_s.at[p], db_r[p].at[m])

    def expert_backward(m):
        for p in range(PARTS):
            w = LANES[p]
            wait_all(disp_b[p].at[m], db_r[p].at[m])
            rows = dot(back[0], chunks(disp_b[p], m, w)).astype(BF16)
            for q in range(4):
                act[:, STARTS[p] + q * w : STARTS[p] + (q + 1) * w] = rows[q * ROWS : (q + 1) * ROWS]
            feats = slice(STARTS[p], STARTS[p] + 4 * w)

            def tile(i, carry):
                hf, at = i // 2, pl.ds(pl.multiple_of((i % 2) * TILE, TILE), TILE)
                to = pl.ds(pl.multiple_of(i * TILE, TILE), TILE)
                a = lax.dot_general(act[:, feats], wd[hf, at, feats], NT, preferred_element_type=F32)
                if p > 0:
                    a = a + acc_a[:, to]
                acc_a[:, to] = a
                return carry

            lax.fori_loop(0, 4, tile, 0)
        a, b, d = gate_pre[m], up_pre[m], acc_a[...]
        sigma = jax.nn.sigmoid(a)
        grad_gate = (d * b * sigma * (1.0 + a * (1.0 - sigma))).astype(BF16)
        grad_up = (d * a * sigma).astype(BF16)
        act[:, : 2 * HALF] = grad_gate
        act[:, 2 * HALF : 4 * HALF] = grad_up
        inv = rms_all[m][:, :1]
        mixed = jnp.sum(grad_gate.astype(F32) * a + grad_up.astype(F32) * b, axis=1, keepdims=True)
        factor = inv * inv * mixed * (1.0 / WIDTH)
        for p in range(PARTS):
            w = LANES[p]
            blocks = []
            for q in range(4):
                cols = slice(STARTS[p] + q * w, STARTS[p] + (q + 1) * w)
                y = jnp.zeros((ROWS, w), F32)
                for n, weights in enumerate((wg, wu)):
                    for hf in range(2):
                        x = act[:, (2 * n + hf) * HALF : (2 * n + hf + 1) * HALF]
                        y = y + lax.dot_general(
                            x, weights[hf, cols, :], NT, preferred_element_type=F32
                        )
                y = y * inv * gain_ref[0:1, cols] - hrows[m, :, cols].astype(F32) * factor
                blocks.append(y.astype(BF16))

            @pl.when(m > 0)
            def _():
                sent(send_cb[p], cb_s.at[p])

            put(send_cb[p], dot(back[1], jnp.concatenate(blocks, axis=0)), w)
            scatter(send_cb[p], coll_b[p], m, cb_s.at[p], cb_r[p].at[m])

    def combine_backward(m):
        gates = jnp.zeros((128, 1), F32)
        for p in range(PARTS):
            w = LANES[p]
            wait_all(coll_b[p].at[m], cb_r[p].at[m])
            upper = gbuf[p][m].astype(F32)
            grads = (upper + dot(pick[m], chunks(coll_b[p], m, w))).astype(BF16)

            @pl.when(s > 0)
            def _():
                @pl.when((m > 0) | (s != 3))
                def _():
                    wait_all(gsend[p], g_ssem.at[p])

                gsend[p][...] = grads
                pltpu.make_async_remote_copy(
                    gsend[p], gbuf[p].at[m], g_ssem.at[p], g_recv[p].at[m],
                    device_id=(s - 1, me), device_id_type=MESH,
                ).start()

            for q in range(4):
                cols = slice(STARTS[p] + q * w, STARTS[p] + (q + 1) * w)
                gin_ref[0, m, :, cols] = grads[q * TOK : (q + 1) * TOK]
            gates = gates + jnp.sum(upper * erows[p][m].astype(F32), axis=1, keepdims=True)
        ggate_ref[0, m] = gates[:TOK] + gates[TOK : 2 * TOK] + gates[2 * TOK : 3 * TOK] + gates[3 * TOK :]

    lag = jnp.where(s == 3, 0, jnp.where(s == 2, 3, 5))

    def when_in(i, step):
        @pl.when((i >= 0) & (i < MICRO))
        def _():
            step(i)

    def tick(j, carry):
        when_in(j - lag, dispatch_backward)
        when_in(j, dispatch_forward)
        when_in(j - 1, combine_forward)
        when_in(j - lag - 1, combine_backward)
        when_in(j, expert_forward)
        when_in(j - lag, expert_backward)
        return carry

    lax.fori_loop(0, MICRO + 6, tick, 0)

    for p in range(PARTS):
        sent(send_df[p], df_s.at[p])
        sent(send_cf[p], cf_s.at[p])
        sent(send_db[p], db_s.at[p])
        sent(send_cb[p], cb_s.at[p])
        wait_all(hsend[p], h_ssem.at[p])
        wait_all(gsend[p], g_ssem.at[p])
    for n in range(3):
        shared[n].wait_send()


def body(tokens_in, cotangent, norm_gain, w_gate, w_up, w_down, expert_ids, gate_weights):
    tiled = jnp.tile(expert_ids[0, :, :, 0], (1, 4))
    gates = jnp.tile(gate_weights[0, :, :, 0], (1, 4))
    vmem = pl.BlockSpec(memory_space=pltpu.VMEM)
    hbm = pl.BlockSpec(memory_space=pl.ANY)
    dma = pltpu.SemaphoreType.DMA

    def parts(make):
        return tuple(make(w) for w in LANES)

    def home(count):
        return parts(lambda w: pltpu.VMEM((count, 128, w), BF16))

    def landing():
        return parts(lambda w: pltpu.VMEM((MICRO, CHIPS, 8, w), BF16))

    def sending():
        return parts(lambda w: pltpu.VMEM((CHIPS, 8, w), BF16))

    def per_micro():
        return tuple(dma((MICRO,)) for w in LANES)

    return pl.pallas_call(
        kernel,
        out_shape=(
            jax.ShapeDtypeStruct((1, MICRO, TOK, WIDTH), BF16),
            jax.ShapeDtypeStruct((1, MICRO, TOK, 1), F32),
        ),
        in_specs=[vmem, vmem, vmem, hbm, hbm, hbm, vmem, vmem, vmem],
        out_specs=(vmem, vmem),
        scratch_shapes=[
            pltpu.VMEM((2, WIDTH, HALF), BF16),
            pltpu.VMEM((2, WIDTH, HALF), BF16),
            pltpu.VMEM((2, HALF, WIDTH), BF16),
            pltpu.VMEM((MICRO, 256, 128), BF16),
            pltpu.VMEM((MICRO, 128, 256), BF16),
            pltpu.VMEM((2, 256, 256), BF16),
            home(MICRO), home(MICRO),
            landing(), landing(), landing(), landing(),
            sending(), sending(), sending(), sending(),
            parts(lambda w: pltpu.VMEM((128, w), BF16)),
            parts(lambda w: pltpu.VMEM((128, w), BF16)),
            home(MICRO),
            pltpu.VMEM((MICRO, ROWS, WIDTH), BF16),
            pltpu.VMEM((MICRO, ROWS, 2 * HALF), F32),
            pltpu.VMEM((MICRO, ROWS, 2 * HALF), F32),
            pltpu.VMEM((MICRO, ROWS, 128), F32),
            pltpu.VMEM((ROWS, 2 * HALF), F32),
            pltpu.VMEM((ROWS, 2 * HALF), F32),
            pltpu.VMEM((ROWS, WIDTH), BF16),
            dma((3,)), dma((3,)), dma((3,)),
            per_micro(), per_micro(), dma((PARTS,)), dma((PARTS,)),
            per_micro(), per_micro(), per_micro(), per_micro(),
            dma((PARTS,)), dma((PARTS,)), dma((PARTS,)), dma((PARTS,)),
        ],
        compiler_params=pltpu.CompilerParams(
            collective_id=0, has_side_effects=True, vmem_limit_bytes=60 * 1024 * 1024
        ),
        cost_estimate=pl.CostEstimate(
            flops=4 * 2 * 6 * 64 * 1024 * WIDTH, bytes_accessed=24 * 1024 * 1024, transcendentals=0
        ),
    )(
        tokens_in, cotangent, norm_gain, w_gate, w_up, w_down,
        tiled[:, None, :], tiled[:, :, None], gates[:, :, None],
    )


def solution(mesh):
    return jax.shard_map(
        body,
        mesh=mesh,
        in_specs=(
            P("section", "expert", None),
            P("section", "expert", None),
            P("section", None),
            P("section", "expert", None, None),
            P("section", "expert", None, None),
            P("section", "expert", None, None),
            P("section", None, "expert", None),
            P("section", None, "expert", None),
        ),
        out_specs=(P("section", None, "expert", None), P("section", None, "expert", None)),
        check_vma=False,
    )
```

time: 1960 us -> 372 us (0.19)
  waiting for transfers between devices: 674 us -> 0 us
  other arithmetic: 489 us -> 0 us
  local copies, waits for them, and re-layouts: 396 us -> 7.64 us
  Pallas kernels: 0 us -> 363 us
  starting transfers between devices: 257 us -> 0 us
  matrix products: 61.6 us -> 0 us
  loops' own time: 31.1 us -> 0 us
  blocking collectives: 28.8 us -> 0 us
    all_to_all x28 -> x0, waiting for transfers between devices: 556 us -> none  [the longest x14 287 us: collect(): lax.all_to_all(flat_rows, 'expert', split_axis=0, concat_axis=0, tiled=True)]
    pallas_call x0 -> x1, Pallas kernels: none -> 363 us  [body(): pl.pallas_call(kernel, out_shape=(jax.ShapeDtypeStruct((1, MICRO, TOK, WI...]
    all_to_all x28 -> x0, starting transfers between devices: 208 us -> none  [the longest x14 106 us: dispatch(): lax.all_to_all(doubled, 'expert', split_axis=0, concat_axis=0, tiled=True)]
    all_to_all x28 -> x0, other arithmetic: 204 us -> none  [the longest x14 102 us: collect(): lax.all_to_all(flat_rows, 'expert', split_axis=0, concat_axis=0, tiled=True)]
    unnamed x181 -> x1, local copies, waits for them, and re-layouts: 165 us -> 2.16 us
    convert_element_type x21 -> x0, other arithmetic: 118 us -> none  [the longest x14 111 us: collect(): returned.reshape(expert_count, 2 * capacity * model_dim).astype(jnp.float32)]
    ppermute x12 -> x0, waiting for transfers between devices: 118 us -> none  [shifted(): return lax.ppermute(block, axis, route)]
    all_to_all x29 -> x0, local copies, waits for them, and re-layouts: 89.5 us -> none  [the longest x15 46 us: dispatch(): lax.all_to_all(doubled, 'expert', split_axis=0, concat_axis=0, tiled=True)]
  transfers between devices with their start and end apart: 40 -> 0, of which waited for: 38 -> 0; matrix products, arithmetic and copies ran while one was open for 8% -> 0% of each run, Pallas kernels for 0% -> 0%
where the time goes in v1:
time: 372 us; the launch traced here: 371 us
  Pallas kernels  363 us (98%)
  local copies, waits for them, and re-layouts  7.64 us (2%)
    pallas_call x1, Pallas kernels, body(): pl.pallas_call(kernel, out_shape=(jax.ShapeDtypeStruct((1, MICRO, TOK, WI...  363 us

profile of v1, /device:TPU:32, one launch (start us, length us, event | category | flops | bytes accessed | tf_op | source)
XLA Modules:
  0.0 371.5 jit_solution(2462437893022397282)
XLA Ops:
  0.6 0.7 tile.21
  1.3 0.7 tile.22.idrow_ref
  2.0 0.7 tile.25
  2.7 1.0 tile.28.gate_ref
  3.6 1.0 tile.27.idcol_ref
  4.6 363.2 %shard_map.95 = (bf16[1,4,32,3584]{3,2,1,0:T(8,128)(2,1)}, f32[1,4,32,1]{3,2,1,0:T(8,128)}) custom-call(bf16[1,32,3584]{2,1,0:T(8,128)(2,1)} %tok_ref.1, bf16[1,32,3584]{2,1,0:T(8,128)(2,1)} %cot_ref.1, f32[1,3584]{1,0:T(1,128)} %gain_ref.1, bf16[1,1,3584,512]{3,2,1,0:T(8,128)(2,1)} %wg_ref.1, bf16[1,1,3584,512]{3,2,1,0:T(8,128)(2,1)} %wu_ref.1, ...), custom_call_target="tpu_custom_call" | custom-call | flops 11274289152 | bytes 25165824 | tf_op jit(solution)/shard_map/pallas_call | solution.py:377
  367.8 1.5 copy.13
  369.3 2.2 copy.15

commit v2 on v1

v2 whole, which is shorter than its diff:
```python
import functools

import jax
import jax.numpy as jnp
from jax import lax
from jax.experimental import pallas as pl
from jax.experimental.pallas import tpu as pltpu
from jax.sharding import PartitionSpec as P

MESH = pl.DeviceIdType.MESH
EPS = 1e-06
MICRO = 4
TOK = 32
CHIPS = 32
WIDTH = 3584
HALF = 512
HIDDEN = 2 * HALF
ROWS = 2 * CHIPS
LANE = 128
PART = 4 * LANE
PARTS = WIDTH // PART
F32 = jnp.float32
BF16 = jnp.bfloat16
NT = (((1,), (1,)), ((), ()))


def iota(shape, dim):
    return lax.broadcasted_iota(jnp.int32, shape, dim)


def dot(a, b):
    return jnp.dot(a, b, preferred_element_type=F32)


def dot_t(a, b):
    return lax.dot_general(a, b, NT, preferred_element_type=F32)


def kernel(
    tok_ref, cot_ref, gain_ref, wg_ref, wu_ref, wd_ref, id_ref, gw_ref,
    gin_ref, ggate_ref,
    wg, wu, wd, place, pick, back, gates,
    hbuf, gbuf, disp_f, disp_b, coll_f, coll_b, send_df, send_db, send_cf, send_cb,
    hsend, gsend, erows, hrows, gate_pre, up_pre, hidden, grad_act, rms_all, acc_a, acc_b, act,
    w_send, w_recv, w_local, h_recv, g_recv, h_ssem, g_ssem,
    df_r, db_r, cf_r, cb_r, df_s, db_s, cf_s, cb_s,
):
    s, me = lax.axis_index("section"), lax.axis_index("expert")
    chip, core = me // 2, me % 2
    cx, cz = chip // 8, chip % 8
    sibling = me + 1 - 2 * core

    columns = [((cx + i) % 4) * 16 + core for i in range(4)]
    layers = [((cz + i) % 8) * 2 for i in range(8)]

    def peer(i):
        return columns[i // 8] + layers[i % 8]

    local = []
    for n, (src, dst) in enumerate(((wg_ref, wg), (wu_ref, wu), (wd_ref, wd))):
        local.append(pltpu.make_async_copy(src.at[0, 0], dst.at[core], w_local.at[n]))
        local[-1].start()

    barrier = pltpu.get_barrier_semaphore()

    for i in range(1, CHIPS):
        pl.semaphore_signal(barrier, inc=1, device_id=(s, peer(i)), device_id_type=MESH)
    pl.semaphore_signal(barrier, inc=1, device_id=(s, sibling), device_id_type=MESH)
    for i in range(1, 4):
        pl.semaphore_signal(barrier, inc=1, device_id=((s + i) % 4, me), device_id_type=MESH)

    def stack(src, dst, p):
        for q in range(4):
            cols = slice(p * PART + q * LANE, p * PART + (q + 1) * LANE)
            dst[p, q * TOK : (q + 1) * TOK, :] = src[0, :, cols]

    for p in range(PARTS):
        @pl.when(s == 0)
        def _():
            stack(tok_ref, hbuf.at[0], p)

        @pl.when(s != 0)
        def _():
            stack(tok_ref, hsend, p)

        @pl.when(s == 3)
        def _():
            stack(cot_ref, gbuf.at[3], p)

        @pl.when(s != 3)
        def _():
            stack(cot_ref, gsend, p)

    def tables(m, carry):
        ti, tj = iota((128, TOK), 0), iota((128, TOK), 1)
        ids = jnp.sum(jnp.where(ti % TOK == tj, id_ref[0, m], 0), axis=1, keepdims=True)
        weights = jnp.sum(jnp.where(ti % TOK == tj, gw_ref[0, m], 0.0), axis=1, keepdims=True)
        gates[m] = jnp.broadcast_to(weights, (128, LANE))
        idcol = jnp.broadcast_to(ids, (128, 128))
        ti, tj = iota((128, 128), 0), iota((128, 128), 1)
        idrow = jnp.sum(jnp.where(ti == tj, idcol, 0), axis=0, keepdims=True)
        same = idcol == idrow
        before_row = same & (ti < TOK) & (ti < tj % TOK)
        before_col = same & (tj < TOK) & (tj < ti % TOK)
        slot_row = 2 * idrow + jnp.sum(before_row.astype(jnp.int32), axis=0, keepdims=True)
        slot_col = 2 * ids + jnp.sum(before_col.astype(jnp.int32), axis=1, keepdims=True)
        r, c = iota((256, 128), 0), iota((256, 128), 1)
        hit = ((r // 8) * 2 + r % 2 == slot_row) & ((r // 2) % 4 == c // TOK)
        place[m] = hit.astype(F32).astype(BF16)
        r, c = iota((128, 256), 1), iota((128, 256), 0)
        hit = ((r // 8) * 2 + r % 2 == slot_col) & ((r // 2) % 4 == c // TOK)
        pick[m] = hit.astype(F32).astype(BF16)
        return carry

    lax.fori_loop(0, MICRO, tables, 0)
    r, c = iota((256, 256), 0), iota((256, 256), 1)
    back[0] = (c == ((r // 2) % 32) * 8 + (r // 64) * 2 + r % 2).astype(F32).astype(BF16)
    back[1] = (r == ((c // 2) % 32) * 8 + (c // 64) * 2 + c % 2).astype(F32).astype(BF16)

    pl.semaphore_wait(barrier, CHIPS + 3)

    def hop(src, dst, ssem, rsem, to):
        pltpu.make_async_remote_copy(
            src, dst, ssem, rsem, device_id=(to, me), device_id_type=MESH
        ).start()

    def bring_tokens(p, carry):
        @pl.when(s != 0)
        def _():
            hop(hsend.at[p], hbuf.at[s, p], h_ssem.at[p], h_recv.at[s, p], 0)

        @pl.when(s != 3)
        def _():
            hop(gsend.at[p], gbuf.at[s, p], g_ssem.at[p], g_recv.at[s, p], 3)

        return carry

    lax.fori_loop(0, PARTS, bring_tokens, 0)

    shared = []
    for n, (src, dst) in enumerate(((wg_ref, wg), (wu_ref, wu), (wd_ref, wd))):
        shared.append(
            pltpu.make_async_remote_copy(
                src.at[0, 0], dst.at[core], w_send.at[n], w_recv.at[n],
                device_id=(s, sibling), device_id_type=MESH,
            )
        )
        shared[-1].start()

    def wait_all(ref, sem):
        pltpu.make_async_copy(ref, ref, sem).wait()

    def others(ref):
        return ref.at[pl.ds(0, CHIPS - 1)]

    def scatter(value, src, dst, ssem, rsem, m, p):
        @pl.when(m > 0)
        def _():
            wait_all(others(src.at[p]), ssem.at[p])

        src[p] = value.reshape(CHIPS, 8, LANE).astype(BF16)

        for i in range(1, CHIPS):
            t = peer(i)
            pltpu.make_async_remote_copy(
                src.at[p, t // 2], dst.at[m, p, chip], ssem.at[p], rsem.at[m, p],
                device_id=(s, t), device_id_type=MESH,
            ).start()
        dst[m, p, chip] = src[p, chip]

    def gathered(ref, sem, m, p):
        wait_all(others(ref.at[m, p]), sem.at[m, p])
        return chunks(ref, m, p)

    def chunks(ref, m, p):
        return ref[m, p].astype(F32).reshape(CHIPS * 8, LANE).astype(BF16)

    def features(p, q=0, size=PART):
        return pl.ds(pl.multiple_of(p * PART + q * LANE, LANE), size)

    def over_parts(step):
        def one(p, carry):
            step(p)
            return carry

        lax.fori_loop(0, PARTS, one, 0)

    def dispatch_forward(m, p):
        @pl.when((s != 0) | (m != 0))
        def _():
            wait_all(hbuf.at[m, p], h_recv.at[m, p])

        scatter(dot(place[m], hbuf[m, p]), send_df, disp_f, df_s, df_r, m, p)

    def expert_forward(m):
        @pl.when(m == 0)
        def _():
            for n in range(2):
                local[n].wait()
                shared[n].wait_recv()

        acc_a[...] = jnp.zeros_like(acc_a)
        acc_b[...] = jnp.zeros_like(acc_b)

        def one(p, total):
            rows = dot(back[0], gathered(disp_f, df_r, m, p))
            for q in range(4):
                block = rows[q * ROWS : (q + 1) * ROWS]
                total = total + block * block
                hrows[m, :, features(p, q, LANE)] = block.astype(BF16)
                act[:, q * LANE : (q + 1) * LANE] = (
                    block * gain_ref[0:1, features(p, q, LANE)]
                ).astype(BF16)
            for hf in range(2):
                to = slice(hf * HALF, (hf + 1) * HALF)
                acc_a[:, to] += dot(act[:, :PART], wg[hf, features(p), :])
                acc_b[:, to] += dot(act[:, :PART], wu[hf, features(p), :])
            return total

        total = lax.fori_loop(0, PARTS, one, jnp.zeros((ROWS, LANE), F32))
        inv = lax.rsqrt(jnp.sum(total, axis=1, keepdims=True) * (1.0 / WIDTH) + EPS)
        rms_all[m] = jnp.broadcast_to(inv, (ROWS, LANE))
        a, b = acc_a[...] * inv, acc_b[...] * inv
        gate_pre[m] = a
        up_pre[m] = b
        hidden[m] = (a * jax.nn.sigmoid(a) * b).astype(BF16)

        @pl.when(m == 0)
        def _():
            @pl.when(s != 3)
            def _():
                local[2].wait()
                shared[2].wait_recv()

    def expert_down(m):
        def one(p):
            y = dot(hidden[m, :, :HALF], wd[0, :, features(p)])
            y = (y + dot(hidden[m, :, HALF:], wd[1, :, features(p)])).astype(BF16)
            y = jnp.concatenate([y[:, q * LANE : (q + 1) * LANE] for q in range(4)], axis=0)
            scatter(dot(back[1], y), send_cf, coll_f, cf_s, cf_r, m, p)

        over_parts(one)

    def combine_forward(m, p):
        rows = dot(pick[m], gathered(coll_f, cf_r, m, p))
        erows[m, p] = rows.astype(BF16)

        @pl.when(s < 3)
        def _():
            @pl.when((m > 0) | (s != 0))
            def _():
                wait_all(hsend.at[p], h_ssem.at[p])

            hsend[p] = (hbuf[m, p].astype(F32) + gates[m] * rows).astype(BF16)
            hop(hsend.at[p], hbuf.at[m, p], h_ssem.at[p], h_recv.at[m, p], s + 1)

    def dispatch_backward(m, p):
        @pl.when((s != 3) | (m != 3))
        def _():
            wait_all(gbuf.at[m, p], g_recv.at[m, p])

        grads = (gates[m] * gbuf[m, p].astype(F32)).astype(BF16)
        scatter(dot(place[m], grads), send_db, disp_b, db_s, db_r, m, p)

    def expert_grad_act(m):
        @pl.when((m == 0) & (s == 3))
        def _():
            local[2].wait()
            shared[2].wait_recv()

        grad_act[m] = jnp.zeros((ROWS, HIDDEN), F32)

        def one(p):
            rows = dot(back[0], gathered(disp_b, db_r, m, p)).astype(BF16)
            for q in range(4):
                act[:, q * LANE : (q + 1) * LANE] = rows[q * ROWS : (q + 1) * ROWS]
            for hf in range(2):
                to = slice(hf * HALF, (hf + 1) * HALF)
                grad_act[m, :, to] += dot_t(act[:, :PART], wd[hf, :, features(p)])

        over_parts(one)

    def expert_backward(m):
        a, b, d = gate_pre[m], up_pre[m], grad_act[m]
        sigma = jax.nn.sigmoid(a)
        grad_gate = (d * b * sigma * (1.0 + a * (1.0 - sigma))).astype(BF16)
        grad_up = (d * a * sigma).astype(BF16)
        act[:, :HIDDEN] = grad_gate
        act[:, HIDDEN : 2 * HIDDEN] = grad_up
        inv = rms_all[m][:, :1]
        mixed = jnp.sum(grad_gate.astype(F32) * a + grad_up.astype(F32) * b, axis=1, keepdims=True)
        factor = inv * inv * mixed * (1.0 / WIDTH)

        def one(p):
            y = jnp.zeros((ROWS, PART), F32)
            for n, weights in enumerate((wg, wu)):
                for hf in range(2):
                    x = act[:, (2 * n + hf) * HALF : (2 * n + hf + 1) * HALF]
                    y = y + dot_t(x, weights[hf, features(p), :])
            y = y * inv * gain_ref[0:1, features(p)] - hrows[m, :, features(p)].astype(F32) * factor
            y = y.astype(BF16)
            y = jnp.concatenate([y[:, q * LANE : (q + 1) * LANE] for q in range(4)], axis=0)
            scatter(dot(back[1], y), send_cb, coll_b, cb_s, cb_r, m, p)

        over_parts(one)

    def combine_backward(m, p):
        delta = dot(pick[m], gathered(coll_b, cb_r, m, p))
        grads = (gbuf[m, p].astype(F32) + delta).astype(BF16)

        @pl.when(s > 0)
        def _():
            @pl.when((m > 0) | (s != 3))
            def _():
                wait_all(gsend.at[p], g_ssem.at[p])

            gsend[p] = grads
            hop(gsend.at[p], gbuf.at[m, p], g_ssem.at[p], g_recv.at[m, p], s - 1)

        for q in range(4):
            gin_ref[0, m, :, features(p, q, LANE)] = grads[q * TOK : (q + 1) * TOK]

    def gate_grads(m):
        def one(p, total):
            return total + gbuf[m, p].astype(F32) * erows[m, p].astype(F32)

        total = lax.fori_loop(0, PARTS, one, jnp.zeros((128, LANE), F32))
        total = total[:TOK] + total[TOK : 2 * TOK] + total[2 * TOK : 3 * TOK] + total[3 * TOK :]
        column = jnp.sum(total, axis=1, keepdims=True)
        diagonal = iota((TOK, TOK), 0) == iota((TOK, TOK), 1)
        ggate_ref[0, m] = jnp.sum(jnp.where(diagonal, column, 0.0), axis=0, keepdims=True)

    def begin(first, second, third, last):
        return jnp.where(s == 0, first, jnp.where(s == 1, second, jnp.where(s == 2, third, last)))

    forward = 4
    grads_in = begin(9, 9, 7, 0)
    grads_out = begin(9, 9, 7, 4)
    down = begin(4, 4, 4, 8)
    home = begin(5, 5, 5, 12)
    scores = begin(10, 10, 8, 12)

    def tick(j, carry):
        def when_in(start, step):
            @pl.when((j >= start) & (j < start + MICRO))
            def _():
                step(lax.rem(j + (16 - start), MICRO))

        def forward_moves(p):
            when_in(home, lambda m: combine_forward(m, p))
            when_in(forward, lambda m: dispatch_forward(m, p))

        def backward_moves(p):
            when_in(grads_out + 1, lambda m: combine_backward(m, p))
            when_in(grads_in, lambda m: dispatch_backward(m, p))

        @pl.when(((j >= forward) & (j <= forward + MICRO)) | (j >= home))
        def _():
            over_parts(forward_moves)

        @pl.when(j >= grads_in)
        def _():
            over_parts(backward_moves)

        when_in(forward, expert_forward)
        when_in(down, expert_down)
        when_in(grads_in, expert_grad_act)
        when_in(grads_out, expert_backward)
        when_in(scores, gate_grads)
        return carry

    lax.fori_loop(0, 16, tick, 0)

    def finish(p):
        for src, sem in ((send_df, df_s), (send_cf, cf_s), (send_db, db_s), (send_cb, cb_s)):
            wait_all(others(src.at[p]), sem.at[p])
        wait_all(hsend.at[p], h_ssem.at[p])
        wait_all(gsend.at[p], g_ssem.at[p])

    over_parts(finish)
    for n in range(3):
        shared[n].wait_send()


def body(tokens_in, cotangent, norm_gain, w_gate, w_up, w_down, expert_ids, gate_weights):
    vmem = pl.BlockSpec(memory_space=pltpu.VMEM)
    hbm = pl.BlockSpec(memory_space=pl.ANY)
    dma = pltpu.SemaphoreType.DMA
    home = pltpu.VMEM((MICRO, PARTS, 128, LANE), BF16)
    landing = pltpu.VMEM((MICRO, PARTS, CHIPS, 8, LANE), BF16)
    sending = pltpu.VMEM((PARTS, CHIPS, 8, LANE), BF16)
    wide = pltpu.VMEM((MICRO, ROWS, HIDDEN), F32)
    each, part = dma((MICRO, PARTS)), dma((PARTS,))
    grad_inputs, grad_gates = pl.pallas_call(
        kernel,
        out_shape=(
            jax.ShapeDtypeStruct((1, MICRO, TOK, WIDTH), BF16),
            jax.ShapeDtypeStruct((1, MICRO, 1, TOK), F32),
        ),
        in_specs=[vmem, vmem, vmem, hbm, hbm, hbm, vmem, vmem],
        out_specs=(vmem, vmem),
        scratch_shapes=[
            pltpu.VMEM((2, WIDTH, HALF), BF16),
            pltpu.VMEM((2, WIDTH, HALF), BF16),
            pltpu.VMEM((2, HALF, WIDTH), BF16),
            pltpu.VMEM((MICRO, 256, 128), BF16),
            pltpu.VMEM((MICRO, 128, 256), BF16),
            pltpu.VMEM((2, 256, 256), BF16),
            pltpu.VMEM((MICRO, 128, LANE), F32),
            home, home,
            landing, landing, landing, landing,
            sending, sending, sending, sending,
            pltpu.VMEM((PARTS, 128, LANE), BF16),
            pltpu.VMEM((PARTS, 128, LANE), BF16),
            home,
            pltpu.VMEM((MICRO, ROWS, WIDTH), BF16),
            wide, wide,
            pltpu.VMEM((MICRO, ROWS, HIDDEN), BF16),
            wide,
            pltpu.VMEM((MICRO, ROWS, LANE), F32),
            pltpu.VMEM((ROWS, HIDDEN), F32),
            pltpu.VMEM((ROWS, HIDDEN), F32),
            pltpu.VMEM((ROWS, 2 * HIDDEN), BF16),
            dma((3,)), dma((3,)), dma((3,)),
            each, each, part, part,
            each, each, each, each,
            part, part, part, part,
        ],
        compiler_params=pltpu.CompilerParams(
            collective_id=0, has_side_effects=True, vmem_limit_bytes=60 * 1024 * 1024
        ),
        cost_estimate=pl.CostEstimate(
            flops=4 * 2 * 6 * 64 * 1024 * WIDTH, bytes_accessed=24 * 1024 * 1024, transcendentals=0
        ),
    )(
        tokens_in, cotangent, norm_gain, w_gate, w_up, w_down,
        jnp.swapaxes(expert_ids, 2, 3), jnp.swapaxes(gate_weights, 2, 3),
    )
    return grad_inputs, jnp.swapaxes(grad_gates, 2, 3)


def solution(mesh):
    return jax.shard_map(
        body,
        mesh=mesh,
        in_specs=(
            P("section", "expert", None),
            P("section", "expert", None),
            P("section", None),
            P("section", "expert", None, None),
            P("section", "expert", None, None),
            P("section", "expert", None, None),
            P("section", None, "expert", None),
            P("section", None, "expert", None),
        ),
        out_specs=(P("section", None, "expert", None), P("section", None, "expert", None)),
        check_vma=False,
    )
```

time: 372 us -> 319 us (0.86)
  Pallas kernels: 363 us -> 315 us
  local copies, waits for them, and re-layouts: 7.64 us -> 3.41 us
    pallas_call x1, Pallas kernels: 363 us -> 315 us  [body(): pl.pallas_call(kernel, out_shape=(jax.ShapeDtypeStruct((1, MICRO, TOK, WI...]
    another operation x5 -> x0, local copies, waits for them, and re-layouts: 3.97 us -> none  [the longest x3 2.32 us: body(): tiled = jnp.tile(expert_ids[0, :, :, 0], (1, 4))]
where the time goes in v2:
time: 319 us
  Pallas kernels  315 us (99%)
  local copies, waits for them, and re-layouts  3.41 us (1%)
    pallas_call x1, Pallas kernels, body(): pl.pallas_call(kernel, out_shape=(jax.ShapeDtypeStruct((1, MICRO, TOK, WI...  315 us

profile of v2, /device:TPU:32, one launch (start us, length us, event | category | flops | bytes accessed | tf_op | source)
XLA Modules:
  0.0 318.9 jit_solution(13630226253641096529)
XLA Ops:
  0.6 314.9 %shard_map.95 = (bf16[1,4,32,3584]{3,2,1,0:T(8,128)(2,1)}, f32[1,4,1,32]{3,2,1,0:T(1,128)}) custom-call(bf16[1,32,3584]{2,1,0:T(8,128)(2,1)} %tok_ref.1, bf16[1,32,3584]{2,1,0:T(8,128)(2,1)} %cot_ref.1, f32[1,3584]{1,0:T(1,128)} %gain_ref.1, bf16[1,1,3584,512]{3,2,1,0:T(8,128)(2,1)} %wg_ref.1, bf16[1,1,3584,512]{3,2,1,0:T(8,128)(2,1)} %wu_ref.1, ...), custom_call_target="tpu_custom_call" | custom-call | flops 11274289152 | bytes 25165824 | tf_op jit(solution)/shard_map/pallas_call | solution.py:394
  315.5 2.2 copy.15
  317.7 1.3 copy.16

commit v3 on v2

--- a/solution.py
+++ b/solution.py
@@ -178,12 +178,12 @@
     def features(p, q=0, size=PART):
         return pl.ds(pl.multiple_of(p * PART + q * LANE, LANE), size)
 
-    def over_parts(step):
+    def over_parts(step, unroll=False):
         def one(p, carry):
             step(p)
             return carry
 
-        lax.fori_loop(0, PARTS, one, 0)
+        lax.fori_loop(0, PARTS, one, 0, unroll=unroll)
 
     def dispatch_forward(m, p):
         @pl.when((s != 0) | (m != 0))
@@ -217,7 +217,7 @@
                 acc_b[:, to] += dot(act[:, :PART], wu[hf, features(p), :])
             return total
 
-        total = lax.fori_loop(0, PARTS, one, jnp.zeros((ROWS, LANE), F32))
+        total = lax.fori_loop(0, PARTS, one, jnp.zeros((ROWS, LANE), F32), unroll=True)
         inv = lax.rsqrt(jnp.sum(total, axis=1, keepdims=True) * (1.0 / WIDTH) + EPS)
         rms_all[m] = jnp.broadcast_to(inv, (ROWS, LANE))
         a, b = acc_a[...] * inv, acc_b[...] * inv
@@ -239,7 +239,7 @@
             y = jnp.concatenate([y[:, q * LANE : (q + 1) * LANE] for q in range(4)], axis=0)
             scatter(dot(back[1], y), send_cf, coll_f, cf_s, cf_r, m, p)
 
-        over_parts(one)
+        over_parts(one, True)
 
     def combine_forward(m, p):
         rows = dot(pick[m], gathered(coll_f, cf_r, m, p))
@@ -278,7 +278,7 @@
                 to = slice(hf * HALF, (hf + 1) * HALF)
                 grad_act[m, :, to] += dot_t(act[:, :PART], wd[hf, :, features(p)])
 
-        over_parts(one)
+        over_parts(one, True)
 
     def expert_backward(m):
         a, b, d = gate_pre[m], up_pre[m], grad_act[m]
@@ -302,7 +302,7 @@
             y = jnp.concatenate([y[:, q * LANE : (q + 1) * LANE] for q in range(4)], axis=0)
             scatter(dot(back[1], y), send_cb, coll_b, cb_s, cb_r, m, p)
 
-        over_parts(one)
+        over_parts(one, True)
 
     def combine_backward(m, p):
         delta = dot(pick[m], gathered(coll_b, cb_r, m, p))
@@ -334,11 +334,12 @@
         return jnp.where(s == 0, first, jnp.where(s == 1, second, jnp.where(s == 2, third, last)))
 
     forward = 4
-    grads_in = begin(9, 9, 7, 0)
-    grads_out = begin(9, 9, 7, 4)
+    tokens_out = begin(3, 4, 4, 4)
+    grads_in = begin(9, 9, 6, 0)
+    grads_out = begin(9, 9, 6, 4)
     down = begin(4, 4, 4, 8)
     home = begin(5, 5, 5, 12)
-    scores = begin(10, 10, 8, 12)
+    scores = begin(10, 10, 7, 12)
 
     def tick(j, carry):
         def when_in(start, step):
@@ -347,14 +348,18 @@
                 step(lax.rem(j + (16 - start), MICRO))
 
         def forward_moves(p):
-            when_in(home, lambda m: combine_forward(m, p))
-            when_in(forward, lambda m: dispatch_forward(m, p))
+            when_in(tokens_out, lambda m: dispatch_forward(m, p))
+
+        def forward_home(m):
+            over_parts(lambda p: combine_forward(m, p))
 
         def backward_moves(p):
             when_in(grads_out + 1, lambda m: combine_backward(m, p))
             when_in(grads_in, lambda m: dispatch_backward(m, p))
 
-        @pl.when(((j >= forward) & (j <= forward + MICRO)) | (j >= home))
+        when_in(home, forward_home)
+
+        @pl.when((j >= tokens_out) & (j <= forward + MICRO))
         def _():
             over_parts(forward_moves)
 

time: 319 us -> 314 us (0.984)
  Pallas kernels: 315 us -> 310 us
    pallas_call x1, Pallas kernels: 315 us -> 310 us  [body(): pl.pallas_call(kernel, out_shape=(jax.ShapeDtypeStruct((1, MICRO, TOK, WI...]
where the time goes in v3:
time: 314 us
  Pallas kernels  310 us (99%)
  local copies, waits for them, and re-layouts  3.41 us (1%)
    pallas_call x1, Pallas kernels, body(): pl.pallas_call(kernel, out_shape=(jax.ShapeDtypeStruct((1, MICRO, TOK, WI...  310 us

profile of v3, /device:TPU:32, one launch (start us, length us, event | category | flops | bytes accessed | tf_op | source)
XLA Modules:
  0.0 314.2 jit_solution(10994955659971420325)
XLA Ops:
  0.6 310.1 %shard_map.95 = (bf16[1,4,32,3584]{3,2,1,0:T(8,128)(2,1)}, f32[1,4,1,32]{3,2,1,0:T(1,128)}) custom-call(bf16[1,32,3584]{2,1,0:T(8,128)(2,1)} %tok_ref.1, bf16[1,32,3584]{2,1,0:T(8,128)(2,1)} %cot_ref.1, f32[1,3584]{1,0:T(1,128)} %gain_ref.1, bf16[1,1,3584,512]{3,2,1,0:T(8,128)(2,1)} %wg_ref.1, bf16[1,1,3584,512]{3,2,1,0:T(8,128)(2,1)} %wu_ref.1, ...), custom_call_target="tpu_custom_call" | custom-call | flops 11274289152 | bytes 25165824 | tf_op jit(solution)/shard_map/pallas_call | solution.py:399
  310.7 2.2 copy.15
  312.9 1.3 copy.16
